TPU v7x, 32 devices: a whole 2x2x4 slice. The times are simulated.
32 devices in a mesh: tm: 16 (over z, x, core), dp: 2 (over y).
Axes of the slice: x: 2, y: 2, z: 4, core: 2. Of those that a mesh axis runs over, the one named last changes fastest.
Arguments:
- queries: bfloat16 [2, 4096, 1024], P('dp', 'tm'), may hold values from -40 to 40
- keys: bfloat16 [2, 4096, 1024], P('dp', 'tm'), may hold values from -40 to 40
- values: bfloat16 [2, 4096, 1024], P('dp', 'tm'), may hold values from -6 to 6
- out_grad: bfloat16 [2, 4096, 1024], P('dp', 'tm'), may hold values from -6 to 6
- temper: float32 [8], replicated, may hold values from 0.5 to 2
Outputs:
- attended: bfloat16 [2, 4096, 1024], P('dp', 'tm')
- query_grad: bfloat16 [2, 4096, 1024], P('dp', 'tm')
- key_grad: bfloat16 [2, 4096, 1024], P('dp', 'tm')
- value_grad: bfloat16 [2, 4096, 1024], P('dp', 'tm')
- temper_grad: float32 [8], replicated
All inputs are finite; a program needn't handle non-finite values.
Results may differ from a plain program's by a relative error of at most 0.0083.
Values may be sent and summed in bfloat16 or wider, within the bound.
No kernel may reach another device: no remote copies, remote signals or barrier semaphores. Data moves between devices by JAX's collectives and lax.ppermute only.
A program may use at most 64 MiB of HBM per device.

v0:
```python
import math

import jax
import jax.numpy as jnp
from jax import lax
from jax.sharding import PartitionSpec as P

HEADS = 8
HEAD_DIM = 128


def from_behind(value, axis, by):
    peers = lax.axis_size(axis)
    pairs = [(i, i + by) for i in range(peers) if 0 <= i + by < peers]
    return lax.ppermute(value, axis, pairs)


def split_heads(array):
    return array.reshape(array.shape[0], array.shape[1], HEADS, HEAD_DIM)


def attend_block(query_rows, key_rows, value_rows, grad_rows, temper, valid):
    batch = query_rows.shape[0]
    length = query_rows.shape[1]
    span = key_rows.shape[1]
    query_heads = split_heads(query_rows)
    key_heads = split_heads(key_rows)
    value_heads = split_heads(value_rows)
    grad_heads = split_heads(grad_rows)
    root = math.sqrt(HEAD_DIM)
    raw_scores = (
        jnp.einsum("sihd,sjhd->shij", query_heads, key_heads, preferred_element_type=jnp.float32)
        / root
    )
    scores = raw_scores * temper[None, :, None, None]
    scores = jnp.where(valid[None, None, None, :], scores, -1e30)
    highest = jnp.max(scores, axis=-1, keepdims=True)
    expo = jnp.exp(scores - highest)
    probs = expo / jnp.sum(expo, axis=-1, keepdims=True)
    probs_low = probs.astype(jnp.bfloat16)
    attended = jnp.einsum(
        "shij,sjhd->sihd", probs_low, value_heads, preferred_element_type=jnp.float32
    )
    attended = attended.reshape(batch, length, -1).astype(jnp.bfloat16)
    prob_grad = jnp.einsum(
        "sihd,sjhd->shij", grad_heads, value_heads, preferred_element_type=jnp.float32
    )
    delta = jnp.sum(probs * prob_grad, axis=-1, keepdims=True)
    score_grad = probs * (prob_grad - delta)
    score_low = score_grad.astype(jnp.bfloat16)
    factor = (temper / root)[None, None, :, None]
    query_grad = (
        jnp.einsum("shij,sjhd->sihd", score_low, key_heads, preferred_element_type=jnp.float32)
        * factor
    )
    query_grad = query_grad.reshape(batch, length, -1).astype(jnp.bfloat16)
    key_part = (
        jnp.einsum("shij,sihd->sjhd", score_low, query_heads, preferred_element_type=jnp.float32)
        * factor
    )
    value_part = jnp.einsum(
        "shij,sihd->sjhd", probs_low, grad_heads, preferred_element_type=jnp.float32
    )
    temper_part = jnp.sum(score_grad * raw_scores, axis=(0, 2, 3))
    key_low = key_part.reshape(batch, span, -1).astype(jnp.bfloat16)
    value_low = value_part.reshape(batch, span, -1).astype(jnp.bfloat16)
    return (attended, query_grad, key_low, value_low, temper_part)


def on_device(queries, keys, values, out_grad, temper):
    length = queries.shape[1]
    device_pos = lax.axis_index("tm")
    nearer = from_behind((keys, values), "tm", 1)
    farther = from_behind((keys, values), "tm", 2)
    key_rows = jnp.concatenate([farther[0], nearer[0], keys], axis=1)
    value_rows = jnp.concatenate([farther[1], nearer[1], values], axis=1)
    valid = device_pos + jnp.arange(3 * length, dtype=jnp.int32) // length - 2 >= 0
    attended, query_grad, key_low, value_low, temper_part = attend_block(
        queries, key_rows, value_rows, out_grad, temper, valid
    )
    key_total = key_low[:, 2 * length :].astype(jnp.float32)
    value_total = value_low[:, 2 * length :].astype(jnp.float32)
    far_back = from_behind((key_low[:, :length], value_low[:, :length]), "tm", -2)
    near_back = from_behind(
        (key_low[:, length : 2 * length], value_low[:, length : 2 * length]), "tm", -1
    )
    key_total = key_total + near_back[0].astype(jnp.float32) + far_back[0].astype(jnp.float32)
    value_total = value_total + near_back[1].astype(jnp.float32) + far_back[1].astype(jnp.float32)
    temper_grad = lax.psum(temper_part, ("tm", "dp"))
    return (
        attended,
        query_grad,
        key_total.astype(jnp.bfloat16),
        value_total.astype(jnp.bfloat16),
        temper_grad,
    )


def solution(mesh):
    in_specs = (
        P("dp", "tm", None),
        P("dp", "tm", None),
        P("dp", "tm", None),
        P("dp", "tm", None),
        P(),
    )
    out_specs = (
        P("dp", "tm", None),
        P("dp", "tm", None),
        P("dp", "tm", None),
        P("dp", "tm", None),
        P(),
    )
    return jax.shard_map(
        on_device, mesh=mesh, in_specs=in_specs, out_specs=out_specs, check_vma=False
    )
```

profile of v0, /device:TPU:11, one launch (start us, length us, event | category | flops | bytes accessed | tf_op | source)
XLA Modules:
  0.0 144.7 jit_solution(11599379929841045480)
XLA Ops:
  0.6 0.0 copy-start.4
  0.7 3.3 %collective-permute-start = (bf16[1,256,1024]{2,1,0:T(8,128)(2,1)}, bf16[1,256,1024]{2,1,0:T(8,128)(2,1)S(1)}, u32[]{:S(2)}, u32[]{:S(2)}) collective-permute-start(bf16[1,256,1024]{2,1,0:T(8,128)(2,1)} %param.7), channel_id=1, source_target_pairs={{0,4},{2,6},{4,8},{6,10},{8,12},{10,14},{12,16},{14,18},{16,20},{1... | collective-permute-start | bytes 1572872 | tf_op jit(solution)/shard_map/ppermute | solution.py:15
  4.0 4.0 %collective-permute-start.1 = (bf16[1,256,1024]{2,1,0:T(8,128)(2,1)}, bf16[1,256,1024]{2,1,0:T(8,128)(2,1)}, u32[]{:S(2)}, u32[]{:S(2)}) collective-permute-start(bf16[1,256,1024]{2,1,0:T(8,128)(2,1)} %param.7), channel_id=1, source_target_pairs={{0,2},{2,4},{4,6},{6,8},{8,10},{10,12},{12,14},{14,16},{16,18},{18... | collective-permute-start | bytes 1572872 | tf_op jit(solution)/shard_map/ppermute | solution.py:15
  7.9 1.2 copy.30
  9.2 1.9 %collective-permute-start.3 = (bf16[1,256,1024]{1,2,0:T(8,128)(2,1)S(1)}, bf16[1,256,1024]{1,2,0:T(8,128)(2,1)}, u32[]{:S(2)}, u32[]{:S(2)}) collective-permute-start(bf16[1,256,1024]{1,2,0:T(8,128)(2,1)S(1)} %copy.30), channel_id=1, source_target_pairs={{0,2},{2,4},{4,6},{6,8},{8,10},{10,12},{12,14},{14,16},{16,18},{18... | collective-permute-start | bytes 1572872 | tf_op jit(solution)/shard_map/ppermute | solution.py:15
  11.1 3.2 %collective-permute-start.2 = (bf16[1,256,1024]{1,2,0:T(8,128)(2,1)S(1)}, bf16[1,256,1024]{1,2,0:T(8,128)(2,1)}, u32[]{:S(2)}, u32[]{:S(2)}) collective-permute-start(bf16[1,256,1024]{1,2,0:T(8,128)(2,1)S(1)} %copy.30), channel_id=1, source_target_pairs={{0,4},{2,6},{4,8},{6,10},{8,12},{10,14},{12,16},{14,18},{16,20},{1... | collective-permute-start | bytes 1572872 | tf_op jit(solution)/shard_map/ppermute | solution.py:15
  14.3 1.2 copy.63
  15.6 0.0 copy-start.1
  15.6 2.2 %copy.64 = bf16[1,256,1024]{1,2,0:T(8,128)(2,1)} copy(bf16[1,256,1024]{2,1,0:T(8,128)(2,1)} %param.8) | data formatting | bytes 1048576 | tf_op jit(solution)/shard_map/reshape.18
  17.8 0.0 collective-permute-done
  17.8 0.0 copy-start.5
  17.8 0.8 copy-done.5
  18.6 7.5 %collective-permute-done.1 = bf16[1,256,1024]{2,1,0:T(8,128)(2,1)} collective-permute-done((bf16[1,256,1024]{2,1,0:T(8,128)(2,1)}, bf16[1,256,1024]{2,1,0:T(8,128)(2,1)}, u32[]{:S(2)}, u32[]{:S(2)}) %collective-permute-start.1) | collective-permute-done | bytes 524320 | tf_op jit(solution)/shard_map/ppermute | solution.py:15
  26.1 1.3 pad_maximum_fusion
  27.4 1.6 %copy.29 = bf16[1,768,1024]{1,2,0:T(8,128)(2,1)} copy(bf16[1,768,1024]{2,1,0:T(8,128)(2,1)S(1)} %pad_maximum_fusion) | data formatting | bytes 3145728 | tf_op jit(solution)/shard_map/concatenate | solution.py:76
  29.0 3.8 %collective-permute-done.3 = bf16[1,256,1024]{1,2,0:T(8,128)(2,1)} collective-permute-done((bf16[1,256,1024]{1,2,0:T(8,128)(2,1)S(1)}, bf16[1,256,1024]{1,2,0:T(8,128)(2,1)}, u32[]{:S(2)}, u32[]{:S(2)}) %collective-permute-start.3) | collective-permute-done | bytes 524320 | tf_op jit(solution)/shard_map/ppermute | solution.py:15
  32.8 6.4 %collective-permute-done.2 = bf16[1,256,1024]{1,2,0:T(8,128)(2,1)} collective-permute-done((bf16[1,256,1024]{1,2,0:T(8,128)(2,1)S(1)}, bf16[1,256,1024]{1,2,0:T(8,128)(2,1)}, u32[]{:S(2)}, u32[]{:S(2)}) %collective-permute-start.2) | collective-permute-done | bytes 524320 | tf_op jit(solution)/shard_map/ppermute | solution.py:15
  39.1 1.3 pad_maximum_fusion.1
  40.4 4.9 %fusion.32 = (f32[8,256]{1,0:T(8,128)S(1)}, f32[8,256,768]{1,2,0:T(8,128)}) fusion(f32[8]{0:T(128)S(1)} %broadcast_multiply_fusion, pred[768]{0:T(1024)(128)(4,1)S(1)} %fusion.25, bf16[768,8,128]{0,2,1:T(8,128)(2,1)S(1)} %bitcast.74, bf16[256,8,128]{0,2,1:T(8,128)(2,1)S(1)} %bitcast.78), kind=kOutput, calls=%fused_computation.46 | convolution fusion | flops 408945408 | bytes 8397600 | tf_op jit(solution)/shard_map/sub | solution.py:38
  45.3 4.0 %fusion.18 = bf16[8,128,256]{2,1,0:T(8,128)(2,1)S(1)} fusion(bf16[768,8,128]{0,2,1:T(8,128)(2,1)} %bitcast.82, f32[8,256,768]{1,2,0:T(8,128)} %get-tuple-element.24, f32[8,256]{1,0:T(8,128)S(1)} %get-tuple-element.23), kind=kOutput, calls=%fused_computation.28 | convolution fusion | flops 406061056 | bytes 8396800 | tf_op jit(solution)/shard_map/shij,sjhd->sihd/dot_general | solution.py:41
  49.4 1.2 copy-done.7
  50.6 1.2 convolution_convert_fusion
  51.7 0.2 copy-done.2
  52.0 3.8 %fusion.2 = (f32[8,256]{1,0:T(8,128)S(1)}, f32[8,768,256]{2,1,0:T(8,128)}) fusion(f32[8,256,768]{1,2,0:T(8,128)S(1)} %copy-done.7, f32[8,256]{1,0:T(8,128)S(1)} %get-tuple-element.23, bf16[768,8,128]{0,2,1:T(8,128)(2,1)S(1)} %bitcast.83, bf16[256,8,128]{0,2,1:T(8,128)(2,1)S(1)} %bitcast.86), kind=kOutput, calls=%fused_computation.5 | convolution fusion | flops 407369728 | bytes 14696448 | tf_op jit(solution)/shard_map/sihd,sjhd->shij/dot_general | solution.py:45
  55.8 1.0 copy.49
  56.8 0.1 fusion.30
  56.9 1.0 copy.60
  57.9 1.0 copy.61
  58.9 1.0 copy.62
  59.9 3.1 %collective-permute-start.7 = (bf16[1,256,1024]{2,1,0:T(8,128)(2,1)}, bf16[1,256,1024]{2,1,0:T(8,128)(2,1)}, u32[]{:S(2)}, u32[]{:S(2)}) collective-permute-start(bf16[1,256,1024]{2,1,0:T(8,128)(2,1)} %copy.62), channel_id=1, source_target_pairs={{4,0},{6,2},{8,4},{10,6},{12,8},{14,10},{16,12},{18,14},{20,16},{2... | collective-permute-start | bytes 1572872 | tf_op jit(solution)/shard_map/ppermute | solution.py:15
  63.0 1.9 %collective-permute-start.6 = (bf16[1,256,1024]{2,1,0:T(8,128)(2,1)}, bf16[1,256,1024]{2,1,0:T(8,128)(2,1)}, u32[]{:S(2)}, u32[]{:S(2)}) collective-permute-start(bf16[1,256,1024]{2,1,0:T(8,128)(2,1)} %copy.61), channel_id=1, source_target_pairs={{2,0},{4,2},{6,4},{8,6},{10,8},{12,10},{14,12},{16,14},{18,16},{20... | collective-permute-start | bytes 1572872 | tf_op jit(solution)/shard_map/ppermute | solution.py:15
  64.9 7.1 %fusion.1 = (f32[8]{0:T(128)S(1)}, bf16[8,256,768]{1,2,0:T(8,128)(2,1)S(1)}) fusion(f32[8,256]{1,0:T(8,128)S(1)} %get-tuple-element.25, f32[8,768,256]{2,1,0:T(8,128)} %get-tuple-element.26, f32[8,256,768]{1,2,0:T(8,128)} %get-tuple-element.24, f32[8,256]{1,0:T(8,128)S(1)} %get-tuple-element.23, bf16[768,8,128]{0,2,1:T(8,128)(2,1)} %bitcast.75, ...), kind=kOutput, calls=%fused_computation.2 | convolution fusion | flops 413663232 | bytes 17842208 | tf_op jit(solution)/shard_map/sihd,sjhd->shij/dot_general | solution.py:32
  72.1 40.5 %psum.7 = f32[8]{0:T(128)} all-reduce(f32[8]{0:T(128)S(1)} %get-tuple-element.15), channel_id=1, replica_groups=mesh['tm'=16,'dp'=2] {'tm','dp'}, use_global_device_ids=true, to_apply=%region_4.5 | all-reduce | flops 8 | bytes 64 | tf_op jit(solution)/shard_map/psum | solution.py:89
  112.6 2.2 %fusion.8 = bf16[1,8,128,768]{3,2,1,0:T(8,128)(2,1)S(1)} fusion(bf16[8,256,768]{1,2,0:T(8,128)(2,1)S(1)} %get-tuple-element.16, bf16[256,8,128]{0,2,1:T(8,128)(2,1)} %bitcast.80, f32[8]{0:T(128)S(1)} %broadcast_multiply_fusion), kind=kOutput, calls=%fused_computation.13 | convolution fusion | flops 404226048 | bytes 5242912 | tf_op jit(solution)/shard_map/shij,sihd->sjhd/dot_general | solution.py:58
  114.8 1.2 fusion.31
  116.0 2.0 %copy.58 = bf16[1,256,1024]{2,1,0:T(8,128)(2,1)} copy(bf16[1,256,1024]{1,2,0:T(8,128)(2,1)} %get-tuple-element.21) | data formatting | bytes 1048576
  118.0 2.0 %copy.59 = bf16[1,256,1024]{2,1,0:T(8,128)(2,1)} copy(bf16[1,256,1024]{1,2,0:T(8,128)(2,1)} %get-tuple-element.22) | data formatting | bytes 1048576
  120.1 1.9 %collective-permute-start.5 = (bf16[1,256,1024]{2,1,0:T(8,128)(2,1)}, bf16[1,256,1024]{2,1,0:T(8,128)(2,1)}, u32[]{:S(2)}, u32[]{:S(2)}) collective-permute-start(bf16[1,256,1024]{2,1,0:T(8,128)(2,1)} %copy.59), channel_id=1, source_target_pairs={{4,0},{6,2},{8,4},{10,6},{12,8},{14,10},{16,12},{18,14},{20,16},{2... | collective-permute-start | bytes 1572872 | tf_op jit(solution)/shard_map/ppermute | solution.py:15
  122.0 3.2 %collective-permute-start.4 = (bf16[1,256,1024]{2,1,0:T(8,128)(2,1)}, bf16[1,256,1024]{2,1,0:T(8,128)(2,1)}, u32[]{:S(2)}, u32[]{:S(2)}) collective-permute-start(bf16[1,256,1024]{2,1,0:T(8,128)(2,1)} %copy.58), channel_id=1, source_target_pairs={{2,0},{4,2},{6,4},{8,6},{10,8},{12,10},{14,12},{16,14},{18,16},{20... | collective-permute-start | bytes 1572872 | tf_op jit(solution)/shard_map/ppermute | solution.py:15
  125.2 2.8 %fusion.17 = bf16[1,8,128,256]{3,2,1,0:T(8,128)(2,1)} fusion(bf16[768,8,128]{0,2,1:T(8,128)(2,1)} %bitcast.76, bf16[8,256,768]{1,2,0:T(8,128)(2,1)S(1)} %get-tuple-element.16, f32[8]{0:T(128)S(1)} %broadcast_multiply_fusion), kind=kOutput, calls=%fused_computation.27 | convolution fusion | flops 403177472 | bytes 5242912 | tf_op jit(solution)/shard_map/shij,sjhd->sihd/dot_general | solution.py:53
  128.0 2.0 %copy.50 = bf16[1,256,1024]{2,1,0:T(8,128)(2,1)} copy(bf16[1,256,1024]{1,2,0:T(8,128)(2,1)} %bitcast.81) | data formatting | bytes 1048576
  130.0 1.2 copy.57
  131.2 0.0 collective-permute-done.7
  131.3 0.0 collective-permute-done.6
  131.3 2.4 %add_convert_fusion = bf16[1,256,1024]{2,1,0:T(8,128)(2,1)} fusion(bf16[1,256,1024]{2,1,0:T(8,128)(2,1)} %collective-permute-done.7, bf16[1,256,1024]{2,1,0:T(8,128)(2,1)} %collective-permute-done.6, bf16[1,256,1024]{2,1,0:T(8,128)(2,1)} %copy.60), kind=kLoop, calls=%fused_computation.29 | loop fusion | flops 1572864 | bytes 2097152 | tf_op jit(solution)/shard_map/convert_element_type | solution.py:94
  133.7 1.6 %collective-permute-done.5 = bf16[1,256,1024]{2,1,0:T(8,128)(2,1)} collective-permute-done((bf16[1,256,1024]{2,1,0:T(8,128)(2,1)}, bf16[1,256,1024]{2,1,0:T(8,128)(2,1)}, u32[]{:S(2)}, u32[]{:S(2)}) %collective-permute-start.5) | collective-permute-done | bytes 524320 | tf_op jit(solution)/shard_map/ppermute | solution.py:15
  135.3 7.1 %collective-permute-done.4 = bf16[1,256,1024]{2,1,0:T(8,128)(2,1)} collective-permute-done((bf16[1,256,1024]{2,1,0:T(8,128)(2,1)}, bf16[1,256,1024]{2,1,0:T(8,128)(2,1)}, u32[]{:S(2)}, u32[]{:S(2)}) %collective-permute-start.4) | collective-permute-done | bytes 524320 | tf_op jit(solution)/shard_map/ppermute | solution.py:15
  142.4 2.3 %add_convert_fusion.1 = bf16[1,256,1024]{2,1,0:T(8,128)(2,1)} fusion(bf16[1,256,1024]{2,1,0:T(8,128)(2,1)} %collective-permute-done.5, bf16[1,256,1024]{2,1,0:T(8,128)(2,1)} %collective-permute-done.4, bf16[1,256,1024]{2,1,0:T(8,128)(2,1)S(1)} %copy.57), kind=kLoop, calls=%fused_computation.30 | loop fusion | flops 1572864 | bytes 2097152 | tf_op jit(solution)/shard_map/convert_element_type | solution.py:93
  (12 shorter events, 0.0 us)
Async XLA Ops:
  0.6 25.5 %copy-start.4 = (bf16[1,256,1024]{2,1,0:T(8,128)(2,1)S(1)}, bf16[1,256,1024]{2,1,0:T(8,128)(2,1)}, u32[]{:S(2)}) copy-start(bf16[1,256,1024]{2,1,0:T(8,128)(2,1)} %param.7) | copy-start | bytes 1572868
  0.6 17.2 %copy-start.6 = (f32[8]{0:T(128)S(1)}, f32[8]{0:T(128)}, u32[]{:S(2)}) copy-start(f32[8]{0:T(128)} %param.9) | copy-start | bytes 100
  0.7 17.2 %collective-permute-start = (bf16[1,256,1024]{2,1,0:T(8,128)(2,1)}, bf16[1,256,1024]{2,1,0:T(8,128)(2,1)S(1)}, u32[]{:S(2)}, u32[]{:S(2)}) collective-permute-start(bf16[1,256,1024]{2,1,0:T(8,128)(2,1)} %param.7), channel_id=1, source_target_pairs={{0,4},{2,6},{4,8},{6,10},{8,12},{10,14},{12,16},{14,18},{16,20},{1... | collective-permute-start | bytes 1572872 | tf_op jit(solution)/shard_map/ppermute | solution.py:15
  4.0 22.1 %collective-permute-start.1 = (bf16[1,256,1024]{2,1,0:T(8,128)(2,1)}, bf16[1,256,1024]{2,1,0:T(8,128)(2,1)}, u32[]{:S(2)}, u32[]{:S(2)}) collective-permute-start(bf16[1,256,1024]{2,1,0:T(8,128)(2,1)} %param.7), channel_id=1, source_target_pairs={{0,2},{2,4},{4,6},{6,8},{8,10},{10,12},{12,14},{14,16},{16,18},{18... | collective-permute-start | bytes 1572872 | tf_op jit(solution)/shard_map/ppermute | solution.py:15
  9.2 23.6 %collective-permute-start.3 = (bf16[1,256,1024]{1,2,0:T(8,128)(2,1)S(1)}, bf16[1,256,1024]{1,2,0:T(8,128)(2,1)}, u32[]{:S(2)}, u32[]{:S(2)}) collective-permute-start(bf16[1,256,1024]{1,2,0:T(8,128)(2,1)S(1)} %copy.30), channel_id=1, source_target_pairs={{0,2},{2,4},{4,6},{6,8},{8,10},{10,12},{12,14},{14,16},{16,18},{18... | collective-permute-start | bytes 1572872 | tf_op jit(solution)/shard_map/ppermute | solution.py:15
  11.1 28.0 %collective-permute-start.2 = (bf16[1,256,1024]{1,2,0:T(8,128)(2,1)S(1)}, bf16[1,256,1024]{1,2,0:T(8,128)(2,1)}, u32[]{:S(2)}, u32[]{:S(2)}) collective-permute-start(bf16[1,256,1024]{1,2,0:T(8,128)(2,1)S(1)} %copy.30), channel_id=1, source_target_pairs={{0,4},{2,6},{4,8},{6,10},{8,12},{10,14},{12,16},{14,18},{16,20},{1... | collective-permute-start | bytes 1572872 | tf_op jit(solution)/shard_map/ppermute | solution.py:15
  15.6 24.9 %copy-start.1 = (bf16[1,256,1024]{1,2,0:T(8,128)(2,1)}, bf16[1,256,1024]{1,2,0:T(8,128)(2,1)S(1)}, u32[]{:S(2)}) copy-start(bf16[1,256,1024]{1,2,0:T(8,128)(2,1)S(1)} %copy.63) | copy-start | bytes 1572868
  17.8 0.8 copy-start.5
  40.4 4.9 %copy-start = (bf16[1,768,1024]{1,2,0:T(8,128)(2,1)}, bf16[1,768,1024]{1,2,0:T(8,128)(2,1)S(1)}, u32[]{:S(2)}) copy-start(bf16[1,768,1024]{1,2,0:T(8,128)(2,1)S(1)} %pad_maximum_fusion.1) | copy-start | bytes 4718596
  45.3 4.1 %copy-start.3 = (bf16[1,256,1024]{1,2,0:T(8,128)(2,1)S(1)}, bf16[1,256,1024]{1,2,0:T(8,128)(2,1)}, u32[]{:S(2)}) copy-start(bf16[1,256,1024]{1,2,0:T(8,128)(2,1)} %copy.64) | copy-start | bytes 1572868
  45.3 5.2 %copy-start.7 = (f32[8,256,768]{1,2,0:T(8,128)S(1)}, f32[8,256,768]{1,2,0:T(8,128)}, u32[]{:S(2)}) copy-start(f32[8,256,768]{1,2,0:T(8,128)} %get-tuple-element.24) | copy-start | bytes 18874372
  50.6 1.4 copy-start.2
  59.9 71.3 %collective-permute-start.7 = (bf16[1,256,1024]{2,1,0:T(8,128)(2,1)}, bf16[1,256,1024]{2,1,0:T(8,128)(2,1)}, u32[]{:S(2)}, u32[]{:S(2)}) collective-permute-start(bf16[1,256,1024]{2,1,0:T(8,128)(2,1)} %copy.62), channel_id=1, source_target_pairs={{4,0},{6,2},{8,4},{10,6},{12,8},{14,10},{16,12},{18,14},{20,16},{2... | collective-permute-start | bytes 1572872 | tf_op jit(solution)/shard_map/ppermute | solution.py:15
  63.0 68.3 %collective-permute-start.6 = (bf16[1,256,1024]{2,1,0:T(8,128)(2,1)}, bf16[1,256,1024]{2,1,0:T(8,128)(2,1)}, u32[]{:S(2)}, u32[]{:S(2)}) collective-permute-start(bf16[1,256,1024]{2,1,0:T(8,128)(2,1)} %copy.61), channel_id=1, source_target_pairs={{2,0},{4,2},{6,4},{8,6},{10,8},{12,10},{14,12},{16,14},{18,16},{20... | collective-permute-start | bytes 1572872 | tf_op jit(solution)/shard_map/ppermute | solution.py:15
  120.1 15.2 %collective-permute-start.5 = (bf16[1,256,1024]{2,1,0:T(8,128)(2,1)}, bf16[1,256,1024]{2,1,0:T(8,128)(2,1)}, u32[]{:S(2)}, u32[]{:S(2)}) collective-permute-start(bf16[1,256,1024]{2,1,0:T(8,128)(2,1)} %copy.59), channel_id=1, source_target_pairs={{4,0},{6,2},{8,4},{10,6},{12,8},{14,10},{16,12},{18,14},{20,16},{2... | collective-permute-start | bytes 1572872 | tf_op jit(solution)/shard_map/ppermute | solution.py:15
  122.0 20.4 %collective-permute-start.4 = (bf16[1,256,1024]{2,1,0:T(8,128)(2,1)}, bf16[1,256,1024]{2,1,0:T(8,128)(2,1)}, u32[]{:S(2)}, u32[]{:S(2)}) collective-permute-start(bf16[1,256,1024]{2,1,0:T(8,128)(2,1)} %copy.58), channel_id=1, source_target_pairs={{2,0},{4,2},{6,4},{8,6},{10,8},{12,10},{14,12},{16,14},{18,16},{20... | collective-permute-start | bytes 1572872 | tf_op jit(solution)/shard_map/ppermute | solution.py:15
where the time goes:
time: 146 us; the launch traced here: 145 us
  blocking collectives  40.5 us (28%)
  waiting for transfers between devices  26.3 us (18%)
  matrix products  26 us (18%)
  starting transfers between devices  22.4 us (15%)
  local copies, waits for them, and re-layouts  21.2 us (15%)
  other arithmetic  7.32 us (5%)
    psum x1, blocking collectives, on_device(): temper_grad = lax.psum(temper_part, ('tm', 'dp'))  40.5 us
    ppermute x8, waiting for transfers between devices, from_behind(): return lax.ppermute(value, axis, pairs)  26.3 us
    ppermute x8, starting transfers between devices, from_behind(): return lax.ppermute(value, axis, pairs)  22.4 us
    unnamed x25, local copies, waits for them, and re-layouts  14.9 us
    dot_general x1, matrix products, attend_block(): jnp.einsum('sihd,sjhd->shij', query_heads, key_heads, preferred_element_t...  7.15 us
    sub x1, matrix products, attend_block(): expo = jnp.exp(scores - highest)  4.9 us
    dot_general x1, matrix products, attend_block(): jnp.einsum('shij,sjhd->sihd', probs_low, value_heads, preferred_element_t...  4.04 us
    dot_general x1, matrix products, attend_block(): jnp.einsum('sihd,sjhd->shij', grad_heads, value_heads, preferred_element_...  3.81 us
  transfers between devices with their start and end apart: 8, of which 5 were waited for; matrix products, arithmetic and copies ran while one was open for 21% of the time, Pallas kernels for 0%

commit v1 on v0

v1 whole, which is shorter than its diff:
```python
import math

import jax
import jax.numpy as jnp
from jax import lax
from jax.experimental import pallas as pl
from jax.experimental.pallas import tpu as pltpu
from jax.sharding import PartitionSpec as P

HEADS = 8
HEAD_DIM = 128
LOG2E = math.log2(math.e)
CHUNKS = (4, 4)
VMEM_LIMIT = 32 * 1024 * 1024


def shift(value, axis, by, parity=None):
    peers = lax.axis_size(axis)
    pairs = [
        (i, i + by)
        for i in range(peers)
        if 0 <= i + by < peers and (parity is None or i % 2 == parity)
    ]
    return lax.ppermute(value, axis, pairs)


def swap(value, axis, mask=1):
    peers = lax.axis_size(axis)
    return lax.ppermute(value, axis, [(i, i ^ mask) for i in range(peers)])


def sum_everywhere(value, axes):
    for axis in axes:
        peers = lax.axis_size(axis)
        if peers & (peers - 1):
            parts = [value]
            for by in range(1, peers):
                pairs = [(i, (i + by) % peers) for i in range(peers)]
                parts.append(lax.ppermute(value, axis, pairs))
            at = lax.axis_index(axis)
            stacked = jnp.roll(jnp.stack(parts[:1] + parts[:0:-1]), at, axis=0)
            value = jnp.sum(stacked, axis=0)
            continue
        mask = 1
        while mask < peers:
            value = value + swap(value, axis, mask)
            mask *= 2
    return value


def pack_kernel(k_ref, v_ref, out_ref):
    out_ref[0] = k_ref[0]
    out_ref[1] = v_ref[0]


def pack(keys, values, first, heads):
    length = keys.shape[1]
    spec = pl.BlockSpec((1, length, HEAD_DIM), lambda i: (0, 0, first + i))
    return pl.pallas_call(
        pack_kernel,
        grid=(heads,),
        in_specs=[spec, spec],
        out_specs=pl.BlockSpec((2, length, HEAD_DIM), lambda i: (0, 0, i)),
        out_shape=jax.ShapeDtypeStruct((2, length, heads * HEAD_DIM), keys.dtype),
        compiler_params=pltpu.CompilerParams(vmem_limit_bytes=VMEM_LIMIT),
        cost_estimate=pl.CostEstimate(
            flops=0, bytes_accessed=8 * length * heads * HEAD_DIM, transcendentals=0
        ),
    )(keys, values)


def dot_nt(a, b):
    return lax.dot_general(a, b, (((1,), (1,)), ((), ())), preferred_element_type=jnp.float32)


def dot_tn(a, b):
    return lax.dot_general(a, b, (((0,), (0,)), ((), ())), preferred_element_type=jnp.float32)


def dot_nn(a, b):
    return jnp.dot(a, b, preferred_element_type=jnp.float32)


def attend_kernel(
    first,
    pos_ref,
    temper_ref,
    q_ref,
    g_ref,
    k_ref,
    v_ref,
    far_ref,
    near_a_ref,
    near_b_ref,
    *refs,
):
    o_ref, dq_ref, own_ref, near_ref, out_far_ref, t_ref = refs[-6:]
    pos = pos_ref[0]
    temper = temper_ref[first + pl.program_id(0)]
    root = math.sqrt(HEAD_DIM)
    factor = temper / root
    scale = factor * LOG2E
    q = q_ref[0]
    g = g_ref[0]
    keys = [far_ref[0], near_a_ref[0] + near_b_ref[0], k_ref[0]]
    values = [far_ref[1], near_a_ref[1] + near_b_ref[1], v_ref[0]]
    lows = [
        jnp.where(pos >= 2, 0.0, -1e30).astype(jnp.float32),
        jnp.where(pos >= 1, 0.0, -1e30).astype(jnp.float32),
        None,
    ]
    scores = []
    for key, low in zip(keys, lows):
        s = dot_nt(key, q) * scale
        scores.append(s if low is None else s + low)
    highest = jnp.max(scores[0], axis=0, keepdims=True)
    for s in scores[1:]:
        highest = jnp.maximum(highest, jnp.max(s, axis=0, keepdims=True))
    expo = [jnp.exp2(s - highest) for s in scores]
    total = sum(jnp.sum(e, axis=0, keepdims=True) for e in expo)
    inverse = 1.0 / total
    probs = [e * inverse for e in expo]
    lows_p = [p.astype(jnp.bfloat16) for p in probs]
    grads = [dot_nt(value, g) for value in values]
    delta = sum(jnp.sum(p * d, axis=0, keepdims=True) for p, d in zip(probs, grads))
    score_grads = [p * (d - delta) for p, d in zip(probs, grads)]
    lows_s = [s.astype(jnp.bfloat16) for s in score_grads]
    row = sum(
        jnp.sum(d * s, axis=0, keepdims=True) for d, s in zip(score_grads, scores)
    )
    t_ref[0] = jnp.broadcast_to(
        jnp.sum(row, axis=1, keepdims=True) / (temper * LOG2E), (1, HEAD_DIM)
    )
    attended = sum(dot_tn(value, p) for value, p in zip(values, lows_p))
    query_grad = sum(dot_tn(key, s) for key, s in zip(keys, lows_s))
    o_ref[0] = attended.T.astype(o_ref.dtype)
    dq_ref[0] = (query_grad * factor).T.astype(dq_ref.dtype)
    for ref, p, s in zip((out_far_ref, near_ref, own_ref), lows_p, lows_s):
        ref[0] = (dot_nn(s, q) * factor).astype(ref.dtype)
        ref[1] = dot_nn(p, g).astype(ref.dtype)


def attend(first, heads, pos, temper, q, g, k, v, far, near_a, near_b, before):
    length = q.shape[1]
    wide = pl.BlockSpec((1, length, HEAD_DIM), lambda i: (0, 0, first + i))
    pair = pl.BlockSpec((2, length, HEAD_DIM), lambda i: (0, 0, i))
    smem = pl.BlockSpec(memory_space=pltpu.SMEM)
    in_specs = [smem, smem, wide, wide, wide, wide, pair, pair, pair]
    args = [pos, temper, q, g, k, v, far, near_a, near_b]
    aliases = {}
    if before is not None:
        aliases = {len(args): 0, len(args) + 1: 1}
        in_specs += [pl.BlockSpec(memory_space=pl.ANY)] * 2
        args += list(before)
    full = jax.ShapeDtypeStruct(q.shape, jnp.bfloat16)
    part = jax.ShapeDtypeStruct((2, length, heads * HEAD_DIM), jnp.bfloat16)
    return pl.pallas_call(
        lambda *refs: attend_kernel(first, *refs),
        grid=(heads,),
        in_specs=in_specs,
        out_specs=[wide, wide, pair, pair, pair, pl.BlockSpec((1, 1, HEAD_DIM), lambda i: (i, 0, 0))],
        out_shape=[full, full, part, part, part, jax.ShapeDtypeStruct((heads, 1, HEAD_DIM), jnp.float32)],
        input_output_aliases=aliases,
        compiler_params=pltpu.CompilerParams(vmem_limit_bytes=VMEM_LIMIT),
        cost_estimate=pl.CostEstimate(
            flops=heads * 18 * 2 * length * length * HEAD_DIM * 3,
            bytes_accessed=heads * 18 * 2 * length * HEAD_DIM,
            transcendentals=heads * 3 * length * length,
        ),
    )(*args)


def finish_kernel(odd_ref, own_ref, near_ref, back_ref, *refs):
    dk_ref, dv_ref = refs[-2:]
    even = odd_ref[0] == 0
    for at, ref in enumerate((dk_ref, dv_ref)):
        near = near_ref[at].astype(jnp.float32)
        near = jnp.where(even, near, jnp.zeros_like(near))
        total = own_ref[at].astype(jnp.float32) + near + back_ref[at].astype(jnp.float32)
        ref[0] = total.astype(ref.dtype)


def finish(first, heads, odd, own, near, back, shape, before):
    length = shape[1]
    wide = pl.BlockSpec((1, length, HEAD_DIM), lambda i: (0, 0, first + i))
    pair = pl.BlockSpec((2, length, HEAD_DIM), lambda i: (0, 0, i))
    in_specs = [pl.BlockSpec(memory_space=pltpu.SMEM), pair, pair, pair]
    args = [odd, own, near, back]
    aliases = {}
    if before is not None:
        aliases = {len(args): 0, len(args) + 1: 1}
        in_specs += [pl.BlockSpec(memory_space=pl.ANY)] * 2
        args += list(before)
    full = jax.ShapeDtypeStruct(shape, jnp.bfloat16)
    return pl.pallas_call(
        finish_kernel,
        grid=(heads,),
        in_specs=in_specs,
        out_specs=[wide, wide],
        out_shape=[full, full],
        input_output_aliases=aliases,
        compiler_params=pltpu.CompilerParams(vmem_limit_bytes=VMEM_LIMIT),
        cost_estimate=pl.CostEstimate(
            flops=0, bytes_accessed=heads * 8 * 2 * length * HEAD_DIM, transcendentals=0
        ),
    )(*args)


def on_device(queries, keys, values, out_grad, temper):
    pos = lax.axis_index("tm").astype(jnp.int32)
    odd = pos % 2
    pos_in, odd_in = pos[None], odd[None]
    starts = [sum(CHUNKS[:i]) for i in range(len(CHUNKS))]
    packed = [pack(keys, values, first, heads) for first, heads in zip(starts, CHUNKS)]
    fars = [shift(both, "tm", 2) for both in packed]
    nears = [shift(both, "tm", 1, parity=0) for both in packed]
    result, grads = None, None
    temper_parts = []
    pending = []
    for at, (first, heads) in enumerate(zip(starts, CHUNKS)):
        passed = shift(fars[at], "tm", -1, parity=1)
        outs = attend(
            first, heads, pos_in, temper, queries, out_grad, keys, values,
            fars[at], nears[at], passed, result,
        )
        result = (outs[0], outs[1])
        own, near, far, temper_part = outs[2:]
        temper_parts.append(temper_part)
        swapped = swap(near, "tm")
        send = jnp.where(
            odd == 1, (far.astype(jnp.float32) + swapped.astype(jnp.float32)).astype(jnp.bfloat16), far
        )
        pending.append((own, swapped, shift(send, "tm", -2)))
    temper_part = jnp.concatenate(temper_parts, axis=0)[:, 0, :]
    temper_grad = sum_everywhere(temper_part, ("tm", "dp"))[:, 0]
    for (first, heads), (own, swapped, back) in zip(zip(starts, CHUNKS), pending):
        grads = finish(first, heads, odd_in, own, swapped, back, keys.shape, grads)
    return (result[0], result[1], grads[0], grads[1], temper_grad)


def solution(mesh):
    rows = P("dp", "tm", None)
    return jax.shard_map(
        on_device,
        mesh=mesh,
        in_specs=(rows, rows, rows, rows, P()),
        out_specs=(rows, rows, rows, rows, P()),
        check_vma=False,
    )
```

time: 146 us -> 98.6 us (0.68)
  the two profiles are of different devices: /device:TPU:11 before, /device:TPU:0 now
where the time goes in v1:
time: 98.6 us; the launch traced here: 98 us
  waiting for transfers between devices  37 us (38%)
  starting transfers between devices  33.1 us (34%)
  Pallas kernels  17.5 us (18%)
  local copies, waits for them, and re-layouts  9.27 us (9%)
    ppermute x7, waiting for transfers between devices, swap(): return lax.ppermute(value, axis, [(i, i ^ mask) for i in range(peers)])  27.3 us
    ppermute x8, starting transfers between devices, shift(): return lax.ppermute(value, axis, pairs)  20.3 us
    pallas_call x2, Pallas kernels, attend(): pl.pallas_call(lambda *refs: attend_kernel(first, *refs), grid=(heads,),...  13.4 us
    ppermute x7, starting transfers between devices, swap(): return lax.ppermute(value, axis, [(i, i ^ mask) for i in range(peers)])  12.8 us
    ppermute x8, waiting for transfers between devices, shift(): return lax.ppermute(value, axis, pairs)  9.72 us
    unnamed x26, local copies, waits for them, and re-layouts  8.64 us
    pallas_call x2, Pallas kernels, finish(): pl.pallas_call(finish_kernel, grid=(heads,), in_specs=in_specs, out_specs...  3.4 us
  transfers between devices with their start and end apart: 15, of which 8 were waited for; matrix products, arithmetic and copies ran while one was open for 1% of the time, Pallas kernels for 16%

profile of v1, /device:TPU:0, one launch (start us, length us, event | category | flops | bytes accessed | tf_op | source)
XLA Modules:
  0.0 98.0 jit_solution(13853816807449056321)
XLA Ops:
  0.6 0.0 copy-start
  0.6 1.0 %copy-done = bf16[1,256,1024]{2,1,0:T(8,128)(2,1)S(1)} copy-done((bf16[1,256,1024]{2,1,0:T(8,128)(2,1)S(1)}, bf16[1,256,1024]{2,1,0:T(8,128)(2,1)}, u32[]{:S(2)}) %copy-start) | copy-done | bytes 524312
  1.7 1.0 %copy-done.2 = bf16[1,256,1024]{2,1,0:T(8,128)(2,1)S(1)} copy-done((bf16[1,256,1024]{2,1,0:T(8,128)(2,1)S(1)}, bf16[1,256,1024]{2,1,0:T(8,128)(2,1)}, u32[]{:S(2)}) %copy-start.2) | copy-done | bytes 524312
  2.7 0.4 shard_map.93
  3.1 0.0 copy-start.1
  3.1 0.0 copy-start.3
  3.1 5.0 %collective-permute-start.3 = (bf16[2,256,512]{2,1,0:T(8,128)(2,1)S(1)}, bf16[2,256,512]{2,1,0:T(8,128)(2,1)S(1)}, u32[]{:S(2)}, u32[]{:S(2)}) collective-permute-start(bf16[2,256,512]{2,1,0:T(8,128)(2,1)S(1)} %shard_map.93), channel_id=1, source_target_pairs={{0,4},{2,6},{4,8},{6,10},{8,12},{10,14},{12,16},{14,18},{16,20},{1... | collective-permute-start | bytes 1572872 | tf_op jit(solution)/shard_map/ppermute | solution.py:24
  8.1 0.4 shard_map.92
  8.5 4.2 %collective-permute-start = (bf16[2,256,512]{2,1,0:T(8,128)(2,1)S(1)}, bf16[2,256,512]{2,1,0:T(8,128)(2,1)}, u32[]{:S(2)}, u32[]{:S(2)}) collective-permute-start(bf16[2,256,512]{2,1,0:T(8,128)(2,1)S(1)} %shard_map.92), channel_id=1, source_target_pairs={{0,4},{2,6},{4,8},{6,10},{8,12},{10,14},{12,16},{14,18},{16,20},{1... | collective-permute-start | bytes 1572872 | tf_op jit(solution)/shard_map/ppermute | solution.py:24
  12.8 1.3 %collective-permute-start.4 = (bf16[2,256,512]{2,1,0:T(8,128)(2,1)S(1)}, bf16[2,256,512]{2,1,0:T(8,128)(2,1)S(1)}, u32[]{:S(2)}, u32[]{:S(2)}) collective-permute-start(bf16[2,256,512]{2,1,0:T(8,128)(2,1)S(1)} %shard_map.93), channel_id=1, source_target_pairs={{0,2},{4,6},{8,10},{12,14},{16,18},{20,22},{24,26},{28,30},{1,3},{... | collective-permute-start | bytes 1572872 | tf_op jit(solution)/shard_map/ppermute | solution.py:24
  14.1 6.3 %collective-permute-done.3.refs_6_ = bf16[2,256,512]{2,1,0:T(8,128)(2,1)S(1)} collective-permute-done((bf16[2,256,512]{2,1,0:T(8,128)(2,1)S(1)}, bf16[2,256,512]{2,1,0:T(8,128)(2,1)S(1)}, u32[]{:S(2)}, u32[]{:S(2)}) %collective-permute-start.3) | collective-permute-done | bytes 524320 | tf_op jit(solution)/shard_map/ppermute | solution.py:24
  20.4 1.3 %collective-permute-start.5 = (bf16[2,256,512]{2,1,0:T(8,128)(2,1)S(1)}, bf16[2,256,512]{2,1,0:T(8,128)(2,1)}, u32[]{:S(2)}, u32[]{:S(2)}) collective-permute-start(bf16[2,256,512]{2,1,0:T(8,128)(2,1)S(1)} %collective-permute-done.3.refs_6_), channel_id=1, source_target_pairs={{2,0},{6,4},{10,8},{14,12},{18,16},{22,20},{26,24},{30,28},{3,1},{... | collective-permute-start | bytes 1572872 | tf_op jit(solution)/shard_map/ppermute | solution.py:24
  21.7 0.0 copy-start.8
  21.7 0.8 copy-done.8
  22.5 4.6 %collective-permute-start.1 = (bf16[2,256,512]{2,1,0:T(8,128)(2,1)S(1)}, bf16[2,256,512]{2,1,0:T(8,128)(2,1)}, u32[]{:S(2)}, u32[]{:S(2)}) collective-permute-start(bf16[2,256,512]{2,1,0:T(8,128)(2,1)S(1)} %shard_map.92), channel_id=1, source_target_pairs={{0,2},{4,6},{8,10},{12,14},{16,18},{20,22},{24,26},{28,30},{1,3},{... | collective-permute-start | bytes 1572872 | tf_op jit(solution)/shard_map/ppermute | solution.py:24
  27.1 3.4 %collective-permute-done.refs_6_ = bf16[2,256,512]{2,1,0:T(8,128)(2,1)} collective-permute-done((bf16[2,256,512]{2,1,0:T(8,128)(2,1)S(1)}, bf16[2,256,512]{2,1,0:T(8,128)(2,1)}, u32[]{:S(2)}, u32[]{:S(2)}) %collective-permute-start) | collective-permute-done | bytes 524320 | tf_op jit(solution)/shard_map/ppermute | solution.py:24
  30.5 1.3 %collective-permute-start.2 = (bf16[2,256,512]{2,1,0:T(8,128)(2,1)}, bf16[2,256,512]{2,1,0:T(8,128)(2,1)}, u32[]{:S(2)}, u32[]{:S(2)}) collective-permute-start(bf16[2,256,512]{2,1,0:T(8,128)(2,1)} %collective-permute-done.refs_6_), channel_id=1, source_target_pairs={{2,0},{6,4},{10,8},{14,12},{18,16},{22,20},{26,24},{30,28},{3,1},{... | collective-permute-start | bytes 1572872 | tf_op jit(solution)/shard_map/ppermute | solution.py:24
  31.8 0.0 copy-start.12
  31.8 0.0 copy-start.10
  31.8 0.8 copy-done.10
  32.6 0.0 copy-start.6
  32.6 1.0 %copy-done.6 = bf16[1,256,1024]{2,1,0:T(8,128)(2,1)S(1)} copy-done((bf16[1,256,1024]{2,1,0:T(8,128)(2,1)S(1)}, bf16[1,256,1024]{2,1,0:T(8,128)(2,1)}, u32[]{:S(2)}) %copy-start.6) | copy-done | bytes 524312
  33.7 1.0 %copy-done.7 = bf16[1,256,1024]{2,1,0:T(8,128)(2,1)S(1)} copy-done((bf16[1,256,1024]{2,1,0:T(8,128)(2,1)S(1)}, bf16[1,256,1024]{2,1,0:T(8,128)(2,1)}, u32[]{:S(2)}) %copy-start.7) | copy-done | bytes 524312
  34.7 1.0 %copy-done.9 = bf16[2,256,512]{2,1,0:T(8,128)(2,1)S(1)} copy-done((bf16[2,256,512]{2,1,0:T(8,128)(2,1)S(1)}, bf16[2,256,512]{2,1,0:T(8,128)(2,1)}, u32[]{:S(2)}) %copy-start.9) | copy-done | bytes 524312
  35.8 1.0 %copy-done.11 = bf16[2,256,512]{2,1,0:T(8,128)(2,1)S(1)} copy-done((bf16[2,256,512]{2,1,0:T(8,128)(2,1)S(1)}, bf16[2,256,512]{2,1,0:T(8,128)(2,1)}, u32[]{:S(2)}) %copy-start.11) | copy-done | bytes 524312
  36.8 6.7 %shard_map.94 = (bf16[1,256,1024]{2,1,0:T(8,128)(2,1)}, bf16[1,256,1024]{2,1,0:T(8,128)(2,1)}, bf16[2,256,512]{2,1,0:T(8,128)(2,1)S(1)}, bf16[2,256,512]{2,1,0:T...) custom-call(s32[1]{0:T(128)} %bitcast.refs_0_, f32[8]{0:T(128)S(1)} %copy-done.12, ...), custom_call_target="tpu_custom_call" | custom-call | flops 3623878656 | bytes 4718592 | tf_op jit(solution)/shard_map/pallas_call | solution.py:157
  43.4 1.9 %collective-permute-start.8 = (bf16[2,256,512]{2,1,0:T(8,128)(2,1)}, bf16[2,256,512]{2,1,0:T(8,128)(2,1)S(1)}, u32[]{:S(2)}, u32[]{:S(2)}) collective-permute-start(bf16[2,256,512]{2,1,0:T(8,128)(2,1)} %get-tuple-element.29), channel_id=1, source_target_pairs={{0,2},{2,0},{4,6},{6,4},{8,10},{10,8},{12,14},{14,12},{16,18},{18,... | collective-permute-start | bytes 1572872 | tf_op jit(solution)/shard_map/ppermute | solution.py:29
  45.4 6.7 %shard_map.95 = (bf16[1,256,1024]{2,1,0:T(8,128)(2,1)}, bf16[1,256,1024]{2,1,0:T(8,128)(2,1)}, bf16[2,256,512]{2,1,0:T(8,128)(2,1)S(1)}, bf16[2,256,512]{2,1,0:T...) custom-call(s32[1]{0:T(128)} %bitcast.refs_0_, ...), custom_call_target="tpu_custom_call", output_to_operand_aliasing={{0}: (9, {}), {1}: (10, {})} | custom-call | flops 3623878656 | bytes 4718592 | tf_op jit(solution)/shard_map/pallas_call | solution.py:157
  52.1 0.8 copy-done.4
  52.9 0.0 collective-permute-start.6
  52.9 0.2 fusion.1
  53.1 1.3 %collective-permute-start.9 = (bf16[2,256,512]{2,1,0:T(8,128)(2,1)S(1)}, bf16[2,256,512]{2,1,0:T(8,128)(2,1)S(1)}, u32[]{:S(2)}, u32[]{:S(2)}) collective-permute-start(bf16[2,256,512]{2,1,0:T(8,128)(2,1)S(1)} %fusion.1), channel_id=1, source_target_pairs={{4,0},{6,2},{8,4},{10,6},{12,8},{14,10},{16,12},{18,14},{20,16},{2... | collective-permute-start | bytes 1572872 | tf_op jit(solution)/shard_map/ppermute | solution.py:24
  54.4 0.6 collective-permute-done.6.near_ref
  55.0 0.2 fusion
  55.2 1.3 %collective-permute-start.7 = (bf16[2,256,512]{2,1,0:T(8,128)(2,1)S(1)}, bf16[2,256,512]{2,1,0:T(8,128)(2,1)S(1)}, u32[]{:S(2)}, u32[]{:S(2)}) collective-permute-start(bf16[2,256,512]{2,1,0:T(8,128)(2,1)S(1)} %fusion), channel_id=1, source_target_pairs={{4,0},{6,2},{8,4},{10,6},{12,8},{14,10},{16,12},{18,14},{20,16},{2... | collective-permute-start | bytes 1572872 | tf_op jit(solution)/shard_map/ppermute | solution.py:24
  56.5 0.2 collective-permute-start.10
  56.7 1.0 %collective-permute-done.10 = f32[8,128]{1,0:T(8,128)S(1)} collective-permute-done((f32[8,128]{1,0:T(8,128)S(1)}, f32[8,128]{1,0:T(8,128)S(1)}, u32[]{:S(2)}, u32[]{:S(2)}) %collective-permute-start.10) | collective-permute-done | bytes 4128 | tf_op jit(solution)/shard_map/ppermute | solution.py:29
  57.7 3.4 %collective-permute-start.11 = (f32[8,128]{1,0:T(8,128)S(1)}, f32[8,128]{1,0:T(8,128)S(1)}, u32[]{:S(2)}, u32[]{:S(2)}) collective-permute-start(f32[8,128]{1,0:T(8,128)S(1)} %add.28), channel_id=1, source_target_pairs={{0,4},{2,6},{4,0},{6,2},{8,12},{10,14},{12,8},{14,10},{16,20},{18,... | collective-permute-start | bytes 12296 | tf_op jit(solution)/shard_map/ppermute | solution.py:29
  61.1 20.4 %collective-permute-done.11 = f32[8,128]{1,0:T(8,128)S(1)} collective-permute-done((f32[8,128]{1,0:T(8,128)S(1)}, f32[8,128]{1,0:T(8,128)S(1)}, u32[]{:S(2)}, u32[]{:S(2)}) %collective-permute-start.11) | collective-permute-done | bytes 4128 | tf_op jit(solution)/shard_map/ppermute | solution.py:29
  81.5 2.7 %collective-permute-start.12 = (f32[8,128]{1,0:T(8,128)S(1)}, f32[8,128]{1,0:T(8,128)S(1)}, u32[]{:S(2)}, u32[]{:S(2)}) collective-permute-start(f32[8,128]{1,0:T(8,128)S(1)} %add.29), channel_id=1, source_target_pairs={{0,8},{2,10},{4,12},{6,14},{8,0},{10,2},{12,4},{14,6},{16,24},{18,... | collective-permute-start | bytes 12296 | tf_op jit(solution)/shard_map/ppermute | solution.py:29
  84.2 1.6 %collective-permute-done.12 = f32[8,128]{1,0:T(8,128)S(1)} collective-permute-done((f32[8,128]{1,0:T(8,128)S(1)}, f32[8,128]{1,0:T(8,128)S(1)}, u32[]{:S(2)}, u32[]{:S(2)}) %collective-permute-start.12) | collective-permute-done | bytes 4128 | tf_op jit(solution)/shard_map/ppermute | solution.py:29
  85.8 3.0 %collective-permute-start.13 = (f32[8,128]{1,0:T(8,128)S(1)}, f32[8,128]{1,0:T(8,128)S(1)}, u32[]{:S(2)}, u32[]{:S(2)}) collective-permute-start(f32[8,128]{1,0:T(8,128)S(1)} %add.30), channel_id=1, source_target_pairs={{0,16},{2,18},{4,20},{6,22},{8,24},{10,26},{12,28},{14,30},{16,0},... | collective-permute-start | bytes 12296 | tf_op jit(solution)/shard_map/ppermute | solution.py:29
  88.8 1.6 %collective-permute-done.13 = f32[8,128]{1,0:T(8,128)S(1)} collective-permute-done((f32[8,128]{1,0:T(8,128)S(1)}, f32[8,128]{1,0:T(8,128)S(1)}, u32[]{:S(2)}, u32[]{:S(2)}) %collective-permute-start.13) | collective-permute-done | bytes 4128 | tf_op jit(solution)/shard_map/ppermute | solution.py:29
  90.4 1.5 %collective-permute-start.14 = (f32[8,128]{1,0:T(8,128)S(1)}, f32[8,128]{1,0:T(8,128)S(1)}, u32[]{:S(2)}, u32[]{:S(2)}) collective-permute-start(f32[8,128]{1,0:T(8,128)S(1)} %add.31), channel_id=1, source_target_pairs={{0,1},{1,0},{2,3},{3,2},{4,5},{5,4},{6,7},{7,6},{8,9},{9,8},{10,11... | collective-permute-start | bytes 12296 | tf_op jit(solution)/shard_map/ppermute | solution.py:29
  91.9 2.1 %collective-permute-done.14 = f32[8,128]{1,0:T(8,128)S(1)} collective-permute-done((f32[8,128]{1,0:T(8,128)S(1)}, f32[8,128]{1,0:T(8,128)S(1)}, u32[]{:S(2)}, u32[]{:S(2)}) %collective-permute-start.14) | collective-permute-done | bytes 4128 | tf_op jit(solution)/shard_map/ppermute | solution.py:29
  94.0 0.6 slice_reduce_fusion
  94.6 1.7 %shard_map.96 = (bf16[1,256,1024]{2,1,0:T(8,128)(2,1)}, bf16[1,256,1024]{2,1,0:T(8,128)(2,1)}) custom-call(s32[1]{0:T(128)} %bitcast.1.odd_ref, bf16[2,256,512]{2,1,0:T(8,128)(2,1)S(1)} %get-tuple-element.28.own_ref, bf16[2,256,512]{2,1,0:T(8,128)(2,1)S(1)} %collective-permute-done.8.near_ref, bf16[2,256,512]{2,1,0:T(8,128)(2,1)S(1)} %collective-permute-done.9.back_ref), custom_call_target="tpu_custom_call" | custom-call | bytes 2097152 | tf_op jit(solution)/shard_map/pallas_call | solution.py:195
  96.3 1.7 %shard_map.97 = (bf16[1,256,1024]{2,1,0:T(8,128)(2,1)}, bf16[1,256,1024]{2,1,0:T(8,128)(2,1)}) custom-call(s32[1]{0:T(128)} %bitcast.1.odd_ref, bf16[2,256,512]{2,1,0:T(8,128)(2,1)S(1)} %copy-done.5, bf16[2,256,512]{2,1,0:T(8,128)(2,1)S(1)} %collective-permute-done.6.near_ref, ...), custom_call_target="tpu_custom_call", output_to_operand_aliasing={{0}: (4, {}), {1}: (5, {})} | custom-call | bytes 2097152 | tf_op jit(solution)/shard_map/pallas_call | solution.py:195
  (23 shorter events, 0.1 us)
Async XLA Ops:
  0.6 1.0 %copy-start = (bf16[1,256,1024]{2,1,0:T(8,128)(2,1)S(1)}, bf16[1,256,1024]{2,1,0:T(8,128)(2,1)}, u32[]{:S(2)}) copy-start(bf16[1,256,1024]{2,1,0:T(8,128)(2,1)} %refs_4_.3) | copy-start | bytes 1572868
  1.7 1.0 %copy-start.2 = (bf16[1,256,1024]{2,1,0:T(8,128)(2,1)S(1)}, bf16[1,256,1024]{2,1,0:T(8,128)(2,1)}, u32[]{:S(2)}) copy-start(bf16[1,256,1024]{2,1,0:T(8,128)(2,1)} %refs_5_.3) | copy-start | bytes 1572868
  3.1 29.5 %copy-start.1 = (bf16[1,256,1024]{2,1,0:T(8,128)(2,1)S(1)}, bf16[1,256,1024]{2,1,0:T(8,128)(2,1)}, u32[]{:S(2)}) copy-start(bf16[1,256,1024]{2,1,0:T(8,128)(2,1)} %refs_4_.3) | copy-start | bytes 1572868
  3.1 29.5 %copy-start.3 = (bf16[1,256,1024]{2,1,0:T(8,128)(2,1)S(1)}, bf16[1,256,1024]{2,1,0:T(8,128)(2,1)}, u32[]{:S(2)}) copy-start(bf16[1,256,1024]{2,1,0:T(8,128)(2,1)} %refs_5_.3) | copy-start | bytes 1572868
  3.1 17.3 %collective-permute-start.3 = (bf16[2,256,512]{2,1,0:T(8,128)(2,1)S(1)}, bf16[2,256,512]{2,1,0:T(8,128)(2,1)S(1)}, u32[]{:S(2)}, u32[]{:S(2)}) collective-permute-start(bf16[2,256,512]{2,1,0:T(8,128)(2,1)S(1)} %shard_map.93), channel_id=1, source_target_pairs={{0,4},{2,6},{4,8},{6,10},{8,12},{10,14},{12,16},{14,18},{16,20},{1... | collective-permute-start | bytes 1572872 | tf_op jit(solution)/shard_map/ppermute | solution.py:24
  8.5 22.0 %collective-permute-start = (bf16[2,256,512]{2,1,0:T(8,128)(2,1)S(1)}, bf16[2,256,512]{2,1,0:T(8,128)(2,1)}, u32[]{:S(2)}, u32[]{:S(2)}) collective-permute-start(bf16[2,256,512]{2,1,0:T(8,128)(2,1)S(1)} %shard_map.92), channel_id=1, source_target_pairs={{0,4},{2,6},{4,8},{6,10},{8,12},{10,14},{12,16},{14,18},{16,20},{1... | collective-permute-start | bytes 1572872 | tf_op jit(solution)/shard_map/ppermute | solution.py:24
  12.8 19.0 %collective-permute-start.4 = (bf16[2,256,512]{2,1,0:T(8,128)(2,1)S(1)}, bf16[2,256,512]{2,1,0:T(8,128)(2,1)S(1)}, u32[]{:S(2)}, u32[]{:S(2)}) collective-permute-start(bf16[2,256,512]{2,1,0:T(8,128)(2,1)S(1)} %shard_map.93), channel_id=1, source_target_pairs={{0,2},{4,6},{8,10},{12,14},{16,18},{20,22},{24,26},{28,30},{1,3},{... | collective-permute-start | bytes 1572872 | tf_op jit(solution)/shard_map/ppermute | solution.py:24
  20.4 12.2 %collective-permute-start.5 = (bf16[2,256,512]{2,1,0:T(8,128)(2,1)S(1)}, bf16[2,256,512]{2,1,0:T(8,128)(2,1)}, u32[]{:S(2)}, u32[]{:S(2)}) collective-permute-start(bf16[2,256,512]{2,1,0:T(8,128)(2,1)S(1)} %collective-permute-done.3.refs_6_), channel_id=1, source_target_pairs={{2,0},{6,4},{10,8},{14,12},{18,16},{22,20},{26,24},{30,28},{3,1},{... | collective-permute-start | bytes 1572872 | tf_op jit(solution)/shard_map/ppermute | solution.py:24
  21.7 0.8 copy-start.8
  22.5 22.9 %collective-permute-start.1 = (bf16[2,256,512]{2,1,0:T(8,128)(2,1)S(1)}, bf16[2,256,512]{2,1,0:T(8,128)(2,1)}, u32[]{:S(2)}, u32[]{:S(2)}) collective-permute-start(bf16[2,256,512]{2,1,0:T(8,128)(2,1)S(1)} %shard_map.92), channel_id=1, source_target_pairs={{0,2},{4,6},{8,10},{12,14},{16,18},{20,22},{24,26},{28,30},{1,3},{... | collective-permute-start | bytes 1572872 | tf_op jit(solution)/shard_map/ppermute | solution.py:24
  30.5 14.9 %collective-permute-start.2 = (bf16[2,256,512]{2,1,0:T(8,128)(2,1)}, bf16[2,256,512]{2,1,0:T(8,128)(2,1)}, u32[]{:S(2)}, u32[]{:S(2)}) collective-permute-start(bf16[2,256,512]{2,1,0:T(8,128)(2,1)} %collective-permute-done.refs_6_), channel_id=1, source_target_pairs={{2,0},{6,4},{10,8},{14,12},{18,16},{22,20},{26,24},{30,28},{3,1},{... | collective-permute-start | bytes 1572872 | tf_op jit(solution)/shard_map/ppermute | solution.py:24
  31.8 0.8 copy-start.12
  31.8 0.8 copy-start.10
  32.6 1.0 %copy-start.6 = (bf16[1,256,1024]{2,1,0:T(8,128)(2,1)S(1)}, bf16[1,256,1024]{2,1,0:T(8,128)(2,1)}, u32[]{:S(2)}) copy-start(bf16[1,256,1024]{2,1,0:T(8,128)(2,1)} %refs_2_.3) | copy-start | bytes 1572868
  33.7 1.0 %copy-start.7 = (bf16[1,256,1024]{2,1,0:T(8,128)(2,1)S(1)}, bf16[1,256,1024]{2,1,0:T(8,128)(2,1)}, u32[]{:S(2)}) copy-start(bf16[1,256,1024]{2,1,0:T(8,128)(2,1)} %refs_3_.3) | copy-start | bytes 1572868
  34.7 1.0 %copy-start.9 = (bf16[2,256,512]{2,1,0:T(8,128)(2,1)S(1)}, bf16[2,256,512]{2,1,0:T(8,128)(2,1)}, u32[]{:S(2)}) copy-start(bf16[2,256,512]{2,1,0:T(8,128)(2,1)} %copy-done.8) | copy-start | bytes 1572868
  35.7 1.0 %copy-start.11 = (bf16[2,256,512]{2,1,0:T(8,128)(2,1)S(1)}, bf16[2,256,512]{2,1,0:T(8,128)(2,1)}, u32[]{:S(2)}) copy-start(bf16[2,256,512]{2,1,0:T(8,128)(2,1)} %copy-done.10) | copy-start | bytes 1572868
  43.4 9.5 %collective-permute-start.8 = (bf16[2,256,512]{2,1,0:T(8,128)(2,1)}, bf16[2,256,512]{2,1,0:T(8,128)(2,1)S(1)}, u32[]{:S(2)}, u32[]{:S(2)}) collective-permute-start(bf16[2,256,512]{2,1,0:T(8,128)(2,1)} %get-tuple-element.29), channel_id=1, source_target_pairs={{0,2},{2,0},{4,6},{6,4},{8,10},{10,8},{12,14},{14,12},{16,18},{18,... | collective-permute-start | bytes 1572872 | tf_op jit(solution)/shard_map/ppermute | solution.py:29
  52.1 0.8 copy-start.4
  52.9 2.1 %collective-permute-start.6 = (bf16[2,256,512]{2,1,0:T(8,128)(2,1)}, bf16[2,256,512]{2,1,0:T(8,128)(2,1)S(1)}, u32[]{:S(2)}, u32[]{:S(2)}) collective-permute-start(bf16[2,256,512]{2,1,0:T(8,128)(2,1)} %get-tuple-element.26), channel_id=1, source_target_pairs={{0,2},{2,0},{4,6},{6,4},{8,10},{10,8},{12,14},{14,12},{16,18},{18,... | collective-permute-start | bytes 1572872 | tf_op jit(solution)/shard_map/ppermute | solution.py:29
  53.1 41.6 %collective-permute-start.9 = (bf16[2,256,512]{2,1,0:T(8,128)(2,1)S(1)}, bf16[2,256,512]{2,1,0:T(8,128)(2,1)S(1)}, u32[]{:S(2)}, u32[]{:S(2)}) collective-permute-start(bf16[2,256,512]{2,1,0:T(8,128)(2,1)S(1)} %fusion.1), channel_id=1, source_target_pairs={{4,0},{6,2},{8,4},{10,6},{12,8},{14,10},{16,12},{18,14},{20,16},{2... | collective-permute-start | bytes 1572872 | tf_op jit(solution)/shard_map/ppermute | solution.py:24
  55.2 41.2 %collective-permute-start.7 = (bf16[2,256,512]{2,1,0:T(8,128)(2,1)S(1)}, bf16[2,256,512]{2,1,0:T(8,128)(2,1)S(1)}, u32[]{:S(2)}, u32[]{:S(2)}) collective-permute-start(bf16[2,256,512]{2,1,0:T(8,128)(2,1)S(1)} %fusion), channel_id=1, source_target_pairs={{4,0},{6,2},{8,4},{10,6},{12,8},{14,10},{16,12},{18,14},{20,16},{2... | collective-permute-start | bytes 1572872 | tf_op jit(solution)/shard_map/ppermute | solution.py:24
  56.5 1.2 %collective-permute-start.10 = (f32[8,128]{1,0:T(8,128)S(1)}, f32[8,128]{1,0:T(8,128)S(1)}, u32[]{:S(2)}, u32[]{:S(2)}) collective-permute-start(f32[8,128]{1,0:T(8,128)S(1)} %bitcast.3), channel_id=1, source_target_pairs={{0,2},{2,0},{4,6},{6,4},{8,10},{10,8},{12,14},{14,12},{16,18},{18,... | collective-permute-start | bytes 12296 | tf_op jit(solution)/shard_map/ppermute | solution.py:29
  57.7 23.7 %collective-permute-start.11 = (f32[8,128]{1,0:T(8,128)S(1)}, f32[8,128]{1,0:T(8,128)S(1)}, u32[]{:S(2)}, u32[]{:S(2)}) collective-permute-start(f32[8,128]{1,0:T(8,128)S(1)} %add.28), channel_id=1, source_target_pairs={{0,4},{2,6},{4,0},{6,2},{8,12},{10,14},{12,8},{14,10},{16,20},{18,... | collective-permute-start | bytes 12296 | tf_op jit(solution)/shard_map/ppermute | solution.py:29
  81.5 4.3 %collective-permute-start.12 = (f32[8,128]{1,0:T(8,128)S(1)}, f32[8,128]{1,0:T(8,128)S(1)}, u32[]{:S(2)}, u32[]{:S(2)}) collective-permute-start(f32[8,128]{1,0:T(8,128)S(1)} %add.29), channel_id=1, source_target_pairs={{0,8},{2,10},{4,12},{6,14},{8,0},{10,2},{12,4},{14,6},{16,24},{18,... | collective-permute-start | bytes 12296 | tf_op jit(solution)/shard_map/ppermute | solution.py:29
  85.8 4.6 %collective-permute-start.13 = (f32[8,128]{1,0:T(8,128)S(1)}, f32[8,128]{1,0:T(8,128)S(1)}, u32[]{:S(2)}, u32[]{:S(2)}) collective-permute-start(f32[8,128]{1,0:T(8,128)S(1)} %add.30), channel_id=1, source_target_pairs={{0,16},{2,18},{4,20},{6,22},{8,24},{10,26},{12,28},{14,30},{16,0},... | collective-permute-start | bytes 12296 | tf_op jit(solution)/shard_map/ppermute | solution.py:29
  90.4 3.6 %collective-permute-start.14 = (f32[8,128]{1,0:T(8,128)S(1)}, f32[8,128]{1,0:T(8,128)S(1)}, u32[]{:S(2)}, u32[]{:S(2)}) collective-permute-start(f32[8,128]{1,0:T(8,128)S(1)} %add.31), channel_id=1, source_target_pairs={{0,1},{1,0},{2,3},{3,2},{4,5},{5,4},{6,7},{7,6},{8,9},{9,8},{10,11... | collective-permute-start | bytes 12296 | tf_op jit(solution)/shard_map/ppermute | solution.py:29
  94.6 1.7 %copy-start.5 = (bf16[2,256,512]{2,1,0:T(8,128)(2,1)S(1)}, bf16[2,256,512]{2,1,0:T(8,128)(2,1)}, u32[]{:S(2)}) copy-start(bf16[2,256,512]{2,1,0:T(8,128)(2,1)} %copy-done.4) | copy-start | bytes 1572868
